TPU v7x, 256 devices: a whole 4x4x8 slice. The times are simulated.
256 devices in a mesh: row: 2 (over core), col: 16 (over y, x), depth: 8 (over z).
Axes of the slice: x: 4, y: 4, z: 8, core: 2. Of those that a mesh axis runs over, the one named last changes fastest.
Arguments:
- tensor: bfloat16 [4096, 128, 2048], P(('row', 'col', 'depth')), may hold values from -6 to 6
- density: bfloat16 [4096, 1024], P(('row', 'col', 'depth')), may hold values from -0.09375 to 0.09375
- tensor_mask: int32 [64, 2, 32], replicated, may hold values 0 or 1
- density_mask: int32 [64, 16], replicated, may hold values 0 or 1
Outputs:
- contracted: bfloat16 [1024, 128, 2048], P('depth', 'row', 'col')
All inputs are finite; a program needn't handle non-finite values.
Results may differ from a plain program's by a relative error of at most 0.017.
Values may be sent and summed in bfloat16 or wider, within the bound.
A program may use at most 192 MiB of HBM per device.

v0:
```python
import jax
import jax.numpy as jnp
from jax import lax
from jax.sharding import PartitionSpec as P

BLK = 64


def body(tensor, density, tensor_mask, density_mask):
    nu_dev, mu_total, aux_total = tensor.shape
    sigma_total = density.shape[1]
    n_dep = lax.axis_size("depth")
    first_row = lax.axis_index(("row", "col", "depth")) * nu_dev
    row_keep = lax.dynamic_slice_in_dim(jnp.repeat(tensor_mask, BLK, axis=0), first_row, nu_dev, 0)
    shaped = tensor.reshape(nu_dev, mu_total // BLK, BLK, aux_total // BLK, BLK)
    tensor_kept = (shaped * row_keep[:, :, None, :, None].astype(tensor.dtype)).reshape(
        nu_dev, mu_total, aux_total
    )
    density_keep = lax.dynamic_slice_in_dim(
        jnp.repeat(density_mask, BLK, axis=0), first_row, nu_dev, 0
    )
    density_kept = (
        density.reshape(nu_dev, sigma_total // BLK, BLK)
        * density_keep[:, :, None].astype(density.dtype)
    ).reshape(nu_dev, sigma_total)
    density_all = lax.all_gather(density_kept, ("row", "col"), axis=0, tiled=True)
    by_aux = lax.all_to_all(tensor_kept, "col", split_axis=2, concat_axis=0, tiled=True)
    remapped = lax.all_to_all(by_aux, "row", split_axis=1, concat_axis=0, tiled=True)
    mu_local = remapped.shape[1]
    aux_local = remapped.shape[2]
    flattened = remapped.reshape(remapped.shape[0], mu_local * aux_local)
    sigma_dev = sigma_total // n_dep
    summed = lax.psum_scatter(
        lax.dot_general(
            density_all, flattened, (((0,), (0,)), ((), ())), preferred_element_type=jnp.float32
        ).astype(jnp.bfloat16),
        "depth",
        scatter_dimension=0,
        tiled=True,
    ).astype(jnp.float32)
    return summed.reshape(sigma_dev, mu_local, aux_local).astype(jnp.bfloat16)


def solution(mesh):
    placed = (P(("row", "col", "depth"), None, None), P(("row", "col", "depth"), None), P(), P())
    return jax.shard_map(
        body, mesh=mesh, in_specs=placed, out_specs=P("depth", "row", "col"), check_vma=False
    )
```

profile of v0, /device:TPU:1, one launch (start us, length us, event | category | flops | bytes accessed | tf_op | source)
XLA Modules:
  0.0 481.7 jit_solution(15140523295629461933)
XLA Ops:
  6.5 1.1 copy.16
  7.7 21.2 %broadcast_in_dim.9 = s32[64,64,2,32]{2,1,0,3:T(8,128)} broadcast(s32[64,2,32]{1,0,2:T(8,128)S(1)} %copy.16), dimensions={0,2,3} | broadcast | bytes 1064960 | tf_op jit(solution)/shard_map/broadcast_in_dim | solution.py:14
  28.9 1.0 dynamic-slice_convert_fusion
  29.8 12.2 %mul.37 = bf16[16,2,64,32,64]{2,1,0,4,3:T(2,128)(2,1)} broadcast(bf16[16,2,32]{1,0,2:T(8,128)(2,1)S(1)} %dynamic-slice_convert_fusion), dimensions={0,1,3} | broadcast | bytes 8390656 | tf_op jit(solution)/shard_map/mul | solution.py:16
  42.0 27.0 %mul.38 = bf16[16,128,2048]{1,0,2:T(8,128)(2,1)} reshape(bf16[16,2,64,32,64]{2,1,0,4,3:T(2,128)(2,1)} %mul.37) | data formatting | bytes 16777216 | tf_op jit(solution)/shard_map/mul | solution.py:16
  69.0 12.5 %copy.17 = bf16[16,128,2048]{1,0,2:T(8,128)(2,1)} copy(bf16[16,128,2048]{2,1,0:T(8,128)(2,1)} %param.4) | data formatting | bytes 16777216 | tf_op args[0]
  81.5 9.6 %mul.39 = bf16[16,128,2048]{1,0,2:T(8,128)(2,1)} multiply(bf16[16,128,2048]{1,0,2:T(8,128)(2,1)} %copy.17, bf16[16,128,2048]{1,0,2:T(8,128)(2,1)} %mul.38) | non-fusion elementwise | flops 4194304 | bytes 25165824 | tf_op jit(solution)/shard_map/mul | solution.py:16
  91.1 0.0 copy-start.1
  91.1 0.0 copy-start
  91.1 7.8 %all-to-all-start = ((bf16[16,128,2048]{1,0,2:T(8,128)(2,1)}), bf16[16,128,2048]{1,0,2:T(8,128)(2,1)}, u32[]{:S(2)}, u32[]{:S(2)}) async-start(bf16[16,128,2048]{1,0,2:T(8,128)(2,1)} %mul.39), calls=%async_computation | async-start | bytes 16777216 | tf_op jit(solution)/shard_map/all_to_all | solution.py:27
  98.8 0.0 all-gather.2.cloned.1.call-start
  98.9 0.0 copy-done.1
  98.9 0.1 copy.15
  99.0 0.1 broadcast_in_dim.8
  99.1 0.1 mul.34
  99.2 0.1 mul.35
  99.4 0.0 copy-done
  99.4 0.6 mul.36
  100.0 0.0 all-gather.2.cloned.1.call-update
  100.0 0.0 reduce-scatter.2.cloned.1.call-start
  100.1 123.8 %all-to-all-done = bf16[16,128,2048]{1,0,2:T(8,128)(2,1)} async-done(((bf16[16,128,2048]{1,0,2:T(8,128)(2,1)}), bf16[16,128,2048]{1,0,2:T(8,128)(2,1)}, u32[]{:S(2)}, u32[]{:S(2)}) %all-to-all-start) | async-done | bytes 8388640 | tf_op jit(solution)/shard_map/all_to_all | solution.py:27
  223.9 12.9 %copy.19 = bf16[16,16,128,128]{3,2,1,0:T(8,128)(2,1)} copy(bf16[16,16,128,128]{2,1,3,0:T(8,128)(2,1)} %bitcast.4) | data formatting | bytes 16777216 | tf_op jit(solution)/shard_map/all_to_all | solution.py:27
  236.8 12.0 %copy.20 = bf16[256,128,128]{2,0,1:T(8,128)(2,1)} copy(bf16[256,128,128]{2,1,0:T(8,128)(2,1)} %bitcast.18) | data formatting | bytes 16777216 | tf_op jit(solution)/shard_map/all_to_all | solution.py:27
  248.8 20.4 %all_to_all.33 = bf16[256,128,128]{2,0,1:T(8,128)(2,1)} all-to-all(bf16[256,128,128]{2,0,1:T(8,128)(2,1)} %copy.20), channel_id=1, replica_groups=mesh['row'=2,'col'=16,'depth'=8] {'row'}, dimensions={1} | all-to-all | bytes 16777216 | tf_op jit(solution)/shard_map/all_to_all | solution.py:28
  269.2 12.0 %copy.21 = bf16[256,2,64,128]{3,2,0,1:T(8,128)(2,1)} copy(bf16[256,2,64,128]{3,0,2,1:T(8,128)(2,1)} %bitcast.19) | data formatting | bytes 16777216 | tf_op jit(solution)/shard_map/all_to_all | solution.py:28
  281.2 0.0 all-gather.2.cloned.1.call-done
  281.2 15.1 %convolution_convert_fusion = bf16[1024,8192]{1,0:T(8,128)(2,1)} fusion(bf16[512,1024]{1,0:T(8,128)(2,1)} %all-gather.2.cloned.1.call-done, bf16[64,8,64,128]{3,2,1,0:T(8,128)(2,1)} %bitcast.20), kind=kOutput, calls=%fused_computation | convolution fusion | flops 8598323200 | bytes 26214400 | tf_op jit(solution)/shard_map/dot_general | solution.py:34
  296.3 0.0 reduce-scatter.2.cloned.1.call-update
  296.3 175.1 %reduce-scatter.2.cloned.1.call-done = bf16[128,8192]{1,0:T(8,128)(2,1)} async-done(((bf16[1024,8192]{1,0:T(8,128)(2,1)}), bf16[128,8192]{1,0:T(8,128)(2,1)}) %reduce-scatter.2.cloned.1.call-update) | async-done | bytes 2097168 | tf_op jit(solution)/shard_map/reduce_scatter | solution.py:33
  471.4 3.5 copy.24
  (1 shorter events, 0.0 us)
Async XLA Ops:
  91.1 7.8 %copy-start.1 = (s32[64,16]{0,1:T(8,128)S(1)}, s32[64,16]{0,1:T(8,128)}, u32[]{:S(2)}) copy-start(s32[64,16]{0,1:T(8,128)} %param.7) | copy-start | bytes 12292
  91.1 8.3 %copy-start = (bf16[16,1024]{1,0:T(8,128)(2,1)S(1)}, bf16[16,1024]{1,0:T(8,128)(2,1)}, u32[]{:S(2)}) copy-start(bf16[16,1024]{1,0:T(8,128)(2,1)} %param.5) | copy-start | bytes 98308
  91.1 132.8 %all-to-all-start = ((bf16[16,128,2048]{1,0,2:T(8,128)(2,1)}), bf16[16,128,2048]{1,0,2:T(8,128)(2,1)}, u32[]{:S(2)}, u32[]{:S(2)}) async-start(bf16[16,128,2048]{1,0,2:T(8,128)(2,1)} %mul.39), calls=%async_computation | async-start | bytes 16777216 | tf_op jit(solution)/shard_map/all_to_all | solution.py:27
  98.8 182.4 %all-gather.2.cloned.1.call-start = ((), (), s32[]{:S(2)}) async-start(), calls=%async_computation.3 | async-start | bytes 1081344 | tf_op jit(solution)/shard_map/all_gather | solution.py:26
  100.0 371.3 %reduce-scatter.2.cloned.1.call-start = ((), (), s32[]{:S(2)}) async-start(), calls=%async_computation.4 | async-start | bytes 18874368 | tf_op jit(solution)/shard_map/reduce_scatter | solution.py:33
Sparse Core Ops, SparseCore 0:
  102.3 128.7 all-gather.1
  296.4 174.8 reduce-scatter.1
where the time goes:
time: 484 us; the launch traced here: 482 us
  waiting for transfers between devices  299 us (62%)
  local copies, waits for them, and re-layouts  115 us (24%)
  blocking collectives  20.4 us (4%)
  matrix products  15.1 us (3%)
  between operations  13.5 us (3%)
  other arithmetic  11.2 us (2%)
  starting transfers between devices  7.85 us (2%)
    reduce_scatter x1, waiting for transfers between devices, body(): lax.psum_scatter(lax.dot_general(density_all, flattened, (((0,), (0,)), (...  175 us
    all_to_all x1, waiting for transfers between devices, body(): lax.all_to_all(tensor_kept, 'col', split_axis=2, concat_axis=0, tiled=True)  124 us
    mul x2, local copies, waits for them, and re-layouts, body(): shaped * row_keep[:, :, None, :, None].astype(tensor.dtype)  39.1 us
    all_to_all x2, local copies, waits for them, and re-layouts, body(): lax.all_to_all(tensor_kept, 'col', split_axis=2, concat_axis=0, tiled=True)  24.9 us
    broadcast_in_dim x1, local copies, waits for them, and re-layouts, body(): jnp.repeat(tensor_mask, BLK, axis=0)  21.2 us
    all_to_all x1, blocking collectives, body(): lax.all_to_all(by_aux, 'row', split_axis=1, concat_axis=0, tiled=True)  20.4 us
    unnamed x8, local copies, waits for them, and re-layouts  17.3 us
    dot_general x1, matrix products, body(): lax.dot_general(density_all, flattened, (((0,), (0,)), ((), ())), preferr...  15.1 us
  transfers between devices with their start and end apart: 3, of which 2 were waited for; matrix products, arithmetic and copies ran while one was open for 8% of the time, Pallas kernels for 0%

commit v1 on v0

v1 whole, which is shorter than its diff:
```python
import functools

import jax
import jax.numpy as jnp
from jax import lax
from jax.experimental import pallas as pl
from jax.experimental.pallas import tpu as pltpu
from jax.sharding import PartitionSpec as P

BLK = 64
MESH = pl.DeviceIdType.MESH
MC = 4
GROUP = 16
BF, F32 = jnp.bfloat16, jnp.float32


def kernel(
    n_row, n_col, n_dep, tensor, density, tmask, dmask, out,
    raw, wide, ready, cols, down, up, first, own_den, den, den_t, total,
    load_sem, den_send, den_recv, x_send, x_recv, z_send, z_recv,
):
    nu, _, mu, aux = tensor.shape
    sigma = density.shape[1]
    per_dev = sigma // n_dep
    half_rows = per_dev // 2
    q_dev = aux // n_col
    chunks = mu // MC
    per_group = GROUP // MC
    hops = n_dep // 2
    peers = n_row * n_col
    row, col, dep = lax.axis_index("row"), lax.axis_index("col"), lax.axis_index("depth")
    me = row * n_col + col
    left, right = lax.rem(dep + n_dep - 1, n_dep), lax.rem(dep + 1, n_dep)
    nu_block = lax.div((me * n_dep + dep) * nu, BLK)
    low = lax.broadcasted_iota(jnp.int32, (nu, 128), 1) < BLK

    def peer(p):
        off = lax.rem(lax.div(p, 2) * 7, n_col)
        pr = lax.rem(row + lax.rem(p, 2), 2)
        y = lax.rem(lax.div(col, 4) + lax.div(off, 4), 4)
        x = lax.rem(lax.rem(col, 4) + lax.rem(off, 4), 4)
        return pr, y * 4 + x

    def load(g):
        return pltpu.make_async_copy(tensor.at[:, :, pl.ds(pl.multiple_of(g * GROUP, GROUP), GROUP), :], raw, load_sem)

    load(0).start()

    for j in range(sigma // 128):
        a = dmask[nu_block, 2 * j].astype(F32)
        b = dmask[nu_block, 2 * j + 1].astype(F32)
        lanes = slice(j * 128, (j + 1) * 128)
        own_den[:, lanes] = (density[:, lanes].astype(F32) * jnp.where(low, a, b)).astype(BF)

    barrier = pltpu.get_barrier_semaphore()

    @pl.loop(1, peers)
    def _(p):
        pr, pc = peer(p)
        pl.semaphore_signal(barrier, inc=1, device_id=(pr, pc, dep), device_id_type=MESH)

    pl.semaphore_signal(barrier, inc=1, device_id=(row, col, left), device_id_type=MESH)
    pl.semaphore_signal(barrier, inc=1, device_id=(row, col, right), device_id_type=MESH)
    pl.semaphore_wait(barrier, peers + 1)

    mine = pl.ds(pl.multiple_of(me * nu, nu), nu)
    pltpu.make_async_copy(own_den, den.at[mine], den_recv).start()

    @pl.loop(1, peers)
    def _(p):
        pr, pc = peer(p)
        pltpu.make_async_remote_copy(
            own_den, den.at[mine], den_send, den_recv, device_id=(pr, pc, dep), device_id_type=MESH
        ).start()

    def prepare(k):
        @pl.when(lax.rem(k, per_group) == 0)
        def _():
            g = lax.div(k, per_group)
            load(g).wait()

            @pl.loop(0, n_col)
            def _(c):
                lanes = pl.ds(pl.multiple_of(c * q_dev, q_dev), q_dev)
                for h in range(n_row):
                    a = tmask[nu_block, h, 2 * c].astype(F32)
                    b = tmask[nu_block, h, 2 * c + 1].astype(F32)
                    keep = jnp.where(low, a, b)[:1][None]
                    part = raw[:, h, :, lanes].astype(F32) * keep
                    wide[h, c] = part.reshape(nu * GROUP, q_dev)

            @pl.when(g + 1 < mu // GROUP)
            def _():
                load(g + 1).start()

        at = lax.rem(k, per_group) * MC

        @pl.loop(0, n_col)
        def _(c):
            for h in range(n_row):
                for j in range(MC):
                    ready[k, h, c, :, j * q_dev : (j + 1) * q_dev] = wide[
                        h, c, pl.ds(at + j, nu, stride=GROUP), :
                    ].astype(BF)

        pltpu.make_async_copy(ready.at[k, row, col], cols.at[k, mine], x_recv.at[k]).start()

        @pl.loop(1, peers)
        def _(p):
            pr, pc = peer(p)
            pltpu.make_async_remote_copy(
                ready.at[k, pr, pc], cols.at[k, mine], x_send.at[k], x_recv.at[k],
                device_id=(pr, pc, dep), device_id_type=MESH,
            ).start()

    def product(k, ahead):
        target = lax.rem(dep + ahead + n_dep, n_dep)
        rows = pl.ds(pl.multiple_of(target * per_dev, per_dev), per_dev)
        return jnp.dot(den_t[rows, :], cols[k], preferred_element_type=F32)

    ways = ((down, right, 1), (up, left, -1))

    def rows_of(w, t):
        if t:
            return slice(None)
        return pl.ds(w * half_rows, half_rows)

    def hop(w, k, t):
        buf, other, _ = ways[w]
        rows = rows_of(w, t)
        src = first.at[k, rows] if t == 0 else buf.at[k, t - 1]
        return pltpu.make_async_remote_copy(
            src, buf.at[k, t, rows], z_send.at[w, k, t], z_recv.at[w, k, t],
            device_id=(row, col, other), device_id_type=MESH,
        )

    def stage(k, t):
        if t == 0:
            pltpu.make_async_copy(cols.at[k], cols.at[k], x_recv.at[k]).wait()
            first[k] = product(k, hops).astype(BF)
            for w in range(2):
                hop(w, k, 0).start()
        elif t < hops:
            for w in range(2):
                buf, _, sign = ways[w]
                mult = product(k, sign * (hops - t))
                hop(w, k, t - 1).wait_recv()
                if t == 1:
                    lo, hi = slice(0, half_rows), slice(half_rows, per_dev)
                    got, fresh = (lo, hi) if w == 0 else (hi, lo)
                    buf[k, 0, got] = (mult[got] + buf[k, 0, got].astype(F32)).astype(BF)
                    buf[k, 0, fresh] = mult[fresh].astype(BF)
                else:
                    buf[k, t - 1] = (mult + buf[k, t - 1].astype(F32)).astype(BF)
                hop(w, k, t).start()
        else:
            mult = product(k, 0)
            for w in range(2):
                hop(w, k, t - 1).wait_recv()
            mult = mult + down[k, t - 1].astype(F32) + up[k, t - 1].astype(F32)
            at = lax.rem(k, per_group) * MC
            for j in range(MC):
                total[pl.ds(at + j, per_dev, stride=GROUP), :] = mult[:, j * q_dev : (j + 1) * q_dev]

            @pl.when(lax.rem(k, per_group) == per_group - 1)
            def _():
                g = pl.ds(pl.multiple_of(lax.div(k, per_group) * GROUP, GROUP), GROUP)

                @pl.loop(0, per_dev // 16)
                def _(s):
                    part = total[pl.ds(pl.multiple_of(s * 16 * GROUP, 16 * GROUP), 16 * GROUP), :]
                    out[pl.ds(s * 16, 16), g, :] = part.reshape(16, GROUP, q_dev).astype(BF)

    prepare(0)
    prepare(1)
    pltpu.make_async_copy(den, den, den_recv).wait()

    @pl.loop(0, n_dep)
    def _(j):
        at = pl.ds(pl.multiple_of(j * per_dev, per_dev), per_dev)
        den_t[at, :] = den[:, at].astype(F32).T.astype(BF)

    @pl.loop(0, chunks + hops)
    def _(i):
        for t in range(hops, -1, -1):
            if t == 0:
                @pl.when(i + 2 < chunks)
                def _():
                    prepare(i + 2)

            @pl.when((i - t >= 0) & (i - t < chunks))
            def _(t=t):
                stage(i - t, t)

    others = pl.ds(0, (peers - 1) * nu)
    pltpu.make_async_copy(den.at[others], den.at[others], den_send).wait()

    @pl.loop(0, chunks)
    def _(k):
        pltpu.make_async_copy(cols.at[k, others], cols.at[k, others], x_send.at[k]).wait()
        for w in range(2):
            for t in range(hops):
                hop(w, k, t).wait_send()


def solution(mesh):
    n_row, n_col, n_dep = (mesh.shape[a] for a in ("row", "col", "depth"))

    def body(tensor, density, tensor_mask, density_mask):
        nu, mu_all, aux = tensor.shape
        sigma = density.shape[1]
        mu, q_dev, per_dev = mu_all // n_row, aux // n_col, sigma // n_dep
        chunks, hops, plane, width = mu // MC, n_dep // 2, nu * n_row * n_col, MC * (aux // n_col)
        vmem, smem = pl.BlockSpec(memory_space=pltpu.VMEM), pl.BlockSpec(memory_space=pltpu.SMEM)
        return pl.pallas_call(
            functools.partial(kernel, n_row, n_col, n_dep),
            out_shape=jax.ShapeDtypeStruct((per_dev, mu, q_dev), BF),
            in_specs=[pl.BlockSpec(memory_space=pl.ANY), vmem, smem, smem],
            out_specs=vmem,
            scratch_shapes=[
                pltpu.VMEM((nu, n_row, GROUP, aux), BF),
                pltpu.VMEM((n_row, n_col, nu * GROUP, q_dev), F32),
                pltpu.VMEM((chunks, n_row, n_col, nu, width), BF),
                pltpu.VMEM((chunks, plane, width), BF),
                pltpu.VMEM((chunks, hops, per_dev, width), BF),
                pltpu.VMEM((chunks, hops, per_dev, width), BF),
                pltpu.VMEM((chunks, per_dev, width), BF),
                pltpu.VMEM((nu, sigma), BF),
                pltpu.VMEM((plane, sigma), BF),
                pltpu.VMEM((sigma, plane), BF),
                pltpu.VMEM((per_dev * GROUP, q_dev), F32),
                pltpu.SemaphoreType.DMA,
                pltpu.SemaphoreType.DMA,
                pltpu.SemaphoreType.DMA,
                pltpu.SemaphoreType.DMA((chunks,)),
                pltpu.SemaphoreType.DMA((chunks,)),
                pltpu.SemaphoreType.DMA((2, chunks, hops)),
                pltpu.SemaphoreType.DMA((2, chunks, hops)),
            ],
            compiler_params=pltpu.CompilerParams(
                collective_id=0, has_side_effects=True, vmem_limit_bytes=58 << 20
            ),
        )(tensor.reshape(nu, n_row, mu, aux), density, tensor_mask, density_mask)

    placed = (P(("row", "col", "depth"), None, None), P(("row", "col", "depth"), None), P(), P())
    return jax.shard_map(
        body, mesh=mesh, in_specs=placed, out_specs=P("depth", "row", "col"), check_vma=False
    )
```

time: 484 us -> 208 us (0.43)
  waiting for transfers between devices: 299 us -> 0 us
  Pallas kernels: 0 us -> 201 us
  local copies, waits for them, and re-layouts: 115 us -> 5.93 us
  blocking collectives: 20.4 us -> 0 us
  matrix products: 15.1 us -> 0 us
  between operations: 13.5 us -> 0.01 us
  other arithmetic: 11.2 us -> 0 us
  starting transfers between devices: 7.85 us -> 0 us
    pallas_call x0 -> x1, Pallas kernels: none -> 201 us  [body(): pl.pallas_call(functools.partial(kernel, n_row, n_col, n_dep), out_shape=...]
    reduce_scatter x1 -> x0, waiting for transfers between devices: 175 us -> none  [body(): lax.psum_scatter(lax.dot_general(density_all, flattened, (((0,), (0,)), (...]
    all_to_all x1 -> x0, waiting for transfers between devices: 124 us -> none  [body(): lax.all_to_all(tensor_kept, 'col', split_axis=2, concat_axis=0, tiled=True)]
    mul x4 -> x0, local copies, waits for them, and re-layouts: 39.3 us -> none  [the longest x2 39.1 us: body(): shaped * row_keep[:, :, None, :, None].astype(tensor.dtype)]
    all_to_all x3 -> x0, local copies, waits for them, and re-layouts: 36.9 us -> none  [the longest x2 24.9 us: body(): lax.all_to_all(tensor_kept, 'col', split_axis=2, concat_axis=0, tiled=True)]
    broadcast_in_dim x2 -> x0, local copies, waits for them, and re-layouts: 21.3 us -> none  [the longest x1 21.2 us: body(): jnp.repeat(tensor_mask, BLK, axis=0)]
    all_to_all x1 -> x0, blocking collectives: 20.4 us -> none  [body(): lax.all_to_all(by_aux, 'row', split_axis=1, concat_axis=0, tiled=True)]
    dot_general x1 -> x0, matrix products: 15.1 us -> none  [body(): lax.dot_general(density_all, flattened, (((0,), (0,)), ((), ())), preferr...]
  transfers between devices with their start and end apart: 3 -> 0, of which waited for: 2 -> 0; matrix products, arithmetic and copies ran while one was open for 8% -> 0% of each run, Pallas kernels for 0% -> 0%
where the time goes in v1:
time: 208 us; the launch traced here: 207 us
  Pallas kernels  201 us (97%)
  local copies, waits for them, and re-layouts  5.93 us (3%)
    pallas_call x1, Pallas kernels, body(): pl.pallas_call(functools.partial(kernel, n_row, n_col, n_dep), out_shape=...  201 us
    unnamed x3, local copies, waits for them, and re-layouts  5.93 us

profile of v1, /device:TPU:1, one launch (start us, length us, event | category | flops | bytes accessed | tf_op | source)
XLA Modules:
  0.0 206.6 jit_solution(5034244491598214087)
XLA Ops:
  0.0 1.4 copy.6.dmask
  1.4 1.5 copy.5.tmask
  2.9 200.6 %shard_map.46 = bf16[128,64,128]{2,1,0:T(8,128)(2,1)} custom-call(bf16[16,2,64,2048]{3,2,1,0:T(8,128)(2,1)} %bitcast.1, bf16[16,1024]{1,0:T(8,128)(2,1)} %density.1, s32[64,2,32]{2,1,0:T(2,128)} %copy.5.tmask, s32[64,16]{1,0:T(8,128)} %copy.6.dmask), custom_call_target="tpu_custom_call" | custom-call | tf_op jit(solution)/shard_map/pallas_call | solution.py:215
  203.5 3.1 %copy.8 = bf16[128,64,128]{2,1,0:T(8,128)(2,1)} copy(bf16[128,64,128]{2,1,0:T(8,128)(2,1)} %shard_map.46) | data formatting | bytes 4194304

commit v2 on v1

v2 whole, which is shorter than its diff:
```python
import functools

import jax
import jax.numpy as jnp
from jax import lax
from jax.experimental import pallas as pl
from jax.experimental.pallas import tpu as pltpu
from jax.sharding import PartitionSpec as P

BLK = 64
MESH = pl.DeviceIdType.MESH
MC = 4
GROUP = 16
LEAD = 2
BF, F32 = jnp.bfloat16, jnp.float32


def kernel(
    n_row, n_col, n_dep, tensor, density, tmask, dmask, out,
    raw, wide, ready, cols, down, up, first, own_den, den, den_t, total,
    load_sem, den_send, den_recv, sib_send, sib_recv, x_send, x_recv, z_send, z_recv,
):
    nu, _, mu, aux = tensor.shape
    per_dev = den.shape[2]
    half_rows = per_dev // 2
    q_dev = aux // n_col
    chunks = mu // MC
    per_group = GROUP // MC
    hops = n_dep // 2
    peers = n_row * n_col
    row, col, dep = lax.axis_index("row"), lax.axis_index("col"), lax.axis_index("depth")
    me = row * n_col + col
    left, right = lax.rem(dep + n_dep - 1, n_dep), lax.rem(dep + 1, n_dep)
    nu_block = lax.div((me * n_dep + dep) * nu, BLK)
    low = lax.broadcasted_iota(jnp.int32, (nu, 128), 1) < BLK
    mine = pl.ds(pl.multiple_of(me * nu, nu), nu)
    same_core = pl.ds(pl.multiple_of(row * n_col * nu, n_col * nu), n_col * nu)

    def peer(p):
        off = lax.rem(lax.div(p, 2) * 7, n_col)
        pr = lax.rem(row + lax.rem(p, 2), 2)
        y = lax.rem(lax.div(col, 4) + lax.div(off, 4), 4)
        x = lax.rem(lax.rem(col, 4) + lax.rem(off, 4), 4)
        return pr, y * 4 + x


    def load(g):
        return pltpu.make_async_copy(tensor.at[:, :, pl.ds(pl.multiple_of(g * GROUP, GROUP), GROUP), :], raw, load_sem)

    def widen(g):
        load(g).wait()

        @pl.loop(0, n_col)
        def _(c):
            lanes = pl.ds(pl.multiple_of(c * q_dev, q_dev), q_dev)
            for h in range(n_row):
                a = tmask[h, 2 * c, nu_block].astype(F32)
                b = tmask[h, 2 * c + 1, nu_block].astype(F32)
                keep = jnp.where(low, a, b)[:1][None]
                part = raw[:, h, :, lanes].astype(F32) * keep
                wide[h, c] = part.reshape(nu * GROUP, q_dev)

    def arrange(k):
        at = lax.rem(k, per_group) * MC

        @pl.loop(0, n_col)
        def _(c):
            for h in range(n_row):
                for j in range(MC):
                    ready[k, h, c, :, j * q_dev : (j + 1) * q_dev] = wide[
                        h, c, pl.ds(at + j, nu, stride=GROUP), :
                    ].astype(BF)

    def send(k):
        pltpu.make_async_copy(ready.at[k, row, col], cols.at[k, mine], x_recv.at[k]).start()

        @pl.loop(1, peers)
        def _(p):
            pr, pc = peer(p)
            pltpu.make_async_remote_copy(
                ready.at[k, pr, pc], cols.at[k, mine], x_send.at[k], x_recv.at[k],
                device_id=(pr, pc, dep), device_id_type=MESH,
            ).start()

    def prepare(k):
        @pl.when(lax.rem(k, per_group) == 0)
        def _():
            g = lax.div(k, per_group)
            widen(g)

            @pl.when(g + 1 < mu // GROUP)
            def _():
                load(g + 1).start()

        arrange(k)
        send(k)


    aheads = [hops] + [s * a for a in range(hops - 1, 0, -1) for s in (1, -1)] + [0]
    needs = [[0]] + [[2 * t - 1, 2 * t] for t in range(1, hops)] + [[n_dep - 1]]

    def block_of(ahead):
        return lax.rem(dep + ahead + n_dep, n_dep)

    def send_den(n):
        b = block_of(aheads[n])
        pltpu.make_async_copy(own_den.at[b], den.at[b, mine], den_recv.at[n]).start()

        @pl.loop(1, n_col)
        def _(p):
            _, pc = peer(2 * p)
            pltpu.make_async_remote_copy(
                own_den.at[b], den.at[b, mine], den_send.at[n], den_recv.at[n],
                device_id=(row, pc, dep), device_id_type=MESH,
            ).start()

    def sibling(n):
        part = den.at[block_of(aheads[n]), same_core]
        return pltpu.make_async_remote_copy(
            part, part, sib_send.at[n], sib_recv.at[n], device_id=(1 - row, col, dep), device_id_type=MESH
        )

    def share_den(n):
        part = den.at[block_of(aheads[n]), same_core]
        pltpu.make_async_copy(part, part, den_recv.at[n]).wait()
        sibling(n).start()

    def turn_den(n):
        b = block_of(aheads[n])
        sibling(n).wait_recv()
        den_t[b] = den[b].astype(F32).T.astype(BF)


    def product(k, ahead):
        return jnp.dot(den_t[block_of(ahead)], cols[k], preferred_element_type=F32)

    ways = ((down, right, 1), (up, left, -1))

    def hop(w, k, t):
        buf, other, _ = ways[w]
        rows = pl.ds(w * half_rows, half_rows) if t == 0 else slice(None)
        src = first.at[k, rows] if t == 0 else buf.at[k, t - 1]
        return pltpu.make_async_remote_copy(
            src, buf.at[k, t, rows], z_send.at[w, k], z_recv.at[w, k, t],
            device_id=(row, col, other), device_id_type=MESH,
        )

    def sent(k):
        rest = pl.ds(0, (peers - 1) * nu)
        pltpu.make_async_copy(cols.at[k, rest], cols.at[k, rest], x_send.at[k]).wait()
        rest = pl.ds(0, hops * per_dev - half_rows)
        for w in range(2):
            pltpu.make_async_copy(cols.at[k, rest], cols.at[k, rest], z_send.at[w, k]).wait()

    def stage(k, t):
        if t == 0:
            pltpu.make_async_copy(cols.at[k], cols.at[k], x_recv.at[k]).wait()
            first[k] = product(k, hops).astype(BF)
            for w in range(2):
                hop(w, k, 0).start()
        elif t < hops:
            for w in range(2):
                buf, _, sign = ways[w]
                mult = product(k, sign * (hops - t))
                hop(w, k, t - 1).wait_recv()
                if t == 1:
                    lo, hi = slice(0, half_rows), slice(half_rows, per_dev)
                    got, fresh = (lo, hi) if w == 0 else (hi, lo)
                    buf[k, 0, got] = (mult[got] + buf[k, 0, got].astype(F32)).astype(BF)
                    buf[k, 0, fresh] = mult[fresh].astype(BF)
                else:
                    buf[k, t - 1] = (mult + buf[k, t - 1].astype(F32)).astype(BF)
                hop(w, k, t).start()
        else:
            mult = product(k, 0)
            for w in range(2):
                hop(w, k, t - 1).wait_recv()
            mult = mult + down[k, t - 1].astype(F32) + up[k, t - 1].astype(F32)
            at = lax.rem(k, per_group) * MC
            for j in range(MC):
                total[pl.ds(at + j, per_dev, stride=GROUP), :] = mult[:, j * q_dev : (j + 1) * q_dev]

            @pl.when(lax.rem(k, per_group) == per_group - 1)
            def _():
                g = pl.ds(pl.multiple_of(lax.div(k, per_group) * GROUP, GROUP), GROUP)

                @pl.loop(0, per_dev // 16)
                def _(s):
                    part = total[pl.ds(pl.multiple_of(s * 16 * GROUP, 16 * GROUP), 16 * GROUP), :]
                    out[pl.ds(s * 16, 16), g, :] = part.reshape(16, GROUP, q_dev).astype(BF)

            @pl.when(k > 0)
            def _():
                sent(k - 1)

    load(0).start()
    for j in range(n_dep * per_dev // 128):
        a = dmask[2 * j, nu_block].astype(F32)
        b = dmask[2 * j + 1, nu_block].astype(F32)
        at = slice(j * 128 % per_dev, j * 128 % per_dev + 128)
        own_den[j * 128 // per_dev, :, at] = (
            density[:, j * 128 : (j + 1) * 128].astype(F32) * jnp.where(low, a, b)
        ).astype(BF)
    widen(0)
    load(1).start()
    for k in range(LEAD):
        arrange(k)

    barrier = pltpu.get_barrier_semaphore()

    @pl.loop(1, peers)
    def _(p):
        pr, pc = peer(p)
        pl.semaphore_signal(barrier, inc=1, device_id=(pr, pc, dep), device_id_type=MESH)

    pl.semaphore_signal(barrier, inc=1, device_id=(row, col, left), device_id_type=MESH)
    pl.semaphore_signal(barrier, inc=1, device_id=(row, col, right), device_id_type=MESH)
    pl.semaphore_wait(barrier, peers + 1)

    for k in range(LEAD):
        for n in needs[k]:
            send_den(n)
        send(k)
    for n in needs[0]:
        share_den(n)

    @pl.loop(0, chunks + hops)
    def _(i):
        for t in range(hops, -1, -1):
            if t == 0:
                for s in range(LEAD, hops + 1):
                    @pl.when(i == s - LEAD)
                    def _(s=s):
                        for n in needs[s]:
                            send_den(n)

                @pl.when(i + LEAD < chunks)
                def _():
                    prepare(i + LEAD)

            @pl.when(i == t)
            def _(t=t):
                for n in needs[t]:
                    turn_den(n)

            @pl.when((i - t >= 0) & (i - t < chunks))
            def _(t=t):
                stage(i - t, t)

        for s in range(1, hops + 1):
            @pl.when(i == s - 1)
            def _(s=s):
                for n in needs[s]:
                    share_den(n)

    sent(chunks - 1)
    rest = pl.ds(0, (n_col - 1) * nu)
    for n in range(n_dep):
        pltpu.make_async_copy(den.at[0, rest], den.at[0, rest], den_send.at[n]).wait()
        sibling(n).wait_send()


def solution(mesh):
    n_row, n_col, n_dep = (mesh.shape[a] for a in ("row", "col", "depth"))

    def body(tensor, density, tensor_mask, density_mask):
        nu, mu_all, aux = tensor.shape
        sigma = density.shape[1]
        mu, q_dev, per_dev = mu_all // n_row, aux // n_col, sigma // n_dep
        chunks, hops, plane, width = mu // MC, n_dep // 2, nu * n_row * n_col, MC * (aux // n_col)
        vmem, smem = pl.BlockSpec(memory_space=pltpu.VMEM), pl.BlockSpec(memory_space=pltpu.SMEM)
        return pl.pallas_call(
            functools.partial(kernel, n_row, n_col, n_dep),
            out_shape=pltpu.VMEM((per_dev, mu, q_dev), BF),
            in_specs=[pl.BlockSpec(memory_space=pl.ANY), vmem, smem, smem],
            out_specs=vmem,
            scratch_shapes=[
                pltpu.VMEM((nu, n_row, GROUP, aux), BF),
                pltpu.VMEM((n_row, n_col, nu * GROUP, q_dev), F32),
                pltpu.VMEM((chunks, n_row, n_col, nu, width), BF),
                pltpu.VMEM((chunks, plane, width), BF),
                pltpu.VMEM((chunks, hops, per_dev, width), BF),
                pltpu.VMEM((chunks, hops, per_dev, width), BF),
                pltpu.VMEM((chunks, per_dev, width), BF),
                pltpu.VMEM((n_dep, nu, per_dev), BF),
                pltpu.VMEM((n_dep, plane, per_dev), BF),
                pltpu.VMEM((n_dep, per_dev, plane), BF),
                pltpu.VMEM((per_dev * GROUP, q_dev), F32),
                pltpu.SemaphoreType.DMA,
                pltpu.SemaphoreType.DMA((n_dep,)),
                pltpu.SemaphoreType.DMA((n_dep,)),
                pltpu.SemaphoreType.DMA((n_dep,)),
                pltpu.SemaphoreType.DMA((n_dep,)),
                pltpu.SemaphoreType.DMA((chunks,)),
                pltpu.SemaphoreType.DMA((chunks,)),
                pltpu.SemaphoreType.DMA((2, chunks)),
                pltpu.SemaphoreType.DMA((2, chunks, hops)),
            ],
            compiler_params=pltpu.CompilerParams(
                collective_id=0, has_side_effects=True, vmem_limit_bytes=54 << 20
            ),
        )(
            tensor.reshape(nu, n_row, mu, aux),
            density,
            tensor_mask.transpose(1, 2, 0),
            density_mask.T,
        )

    placed = (P(("row", "col", "depth"), None, None), P(("row", "col", "depth"), None), P(), P())
    return jax.shard_map(
        body, mesh=mesh, in_specs=placed, out_specs=P("depth", "row", "col"), check_vma=False
    )
```

time: 208 us -> 196 us (0.942)
  Pallas kernels: 201 us -> 194 us
  local copies, waits for them, and re-layouts: 5.93 us -> 1.32 us
    pallas_call x1, Pallas kernels: 201 us -> 194 us  [body(): pl.pallas_call(functools.partial(kernel, n_row, n_col, n_dep), out_shape=...]
    unnamed x3 -> x1, local copies, waits for them, and re-layouts: 5.93 us -> 1.32 us
where the time goes in v2:
time: 196 us; the launch traced here: 195 us
  Pallas kernels  194 us (99%)
    pallas_call x1, Pallas kernels, body(): pl.pallas_call(functools.partial(kernel, n_row, n_col, n_dep), out_shape=...  194 us

profile of v2, /device:TPU:1, one launch (start us, length us, event | category | flops | bytes accessed | tf_op | source)
XLA Modules:
  0.0 195.4 jit_solution(13485539926262384201)
XLA Ops:
  0.0 194.1 %shard_map.46 = bf16[128,64,128]{2,1,0:T(8,128)(2,1)S(1)} custom-call(bf16[16,2,64,2048]{3,2,1,0:T(8,128)(2,1)} %bitcast.3, bf16[16,1024]{1,0:T(8,128)(2,1)} %density.1, s32[2,32,64]{2,1,0:T(8,128)} %bitcast.4, s32[16,64]{1,0:T(8,128)} %bitcast.5), custom_call_target="tpu_custom_call" | custom-call | tf_op jit(solution)/shard_map/pallas_call | solution.py:272
  194.1 1.3 copy.6

commit v3 on v2

--- a/solution.py
+++ b/solution.py
@@ -194,6 +194,15 @@
                 sent(k - 1)
 
     load(0).start()
+    barrier = pltpu.get_barrier_semaphore()
+
+    @pl.loop(1, peers)
+    def _(p):
+        pr, pc = peer(p)
+        pl.semaphore_signal(barrier, inc=1, device_id=(pr, pc, dep), device_id_type=MESH)
+
+    pl.semaphore_signal(barrier, inc=1, device_id=(row, col, left), device_id_type=MESH)
+    pl.semaphore_signal(barrier, inc=1, device_id=(row, col, right), device_id_type=MESH)
     for j in range(n_dep * per_dev // 128):
         a = dmask[2 * j, nu_block].astype(F32)
         b = dmask[2 * j + 1, nu_block].astype(F32)
@@ -201,30 +210,19 @@
         own_den[j * 128 // per_dev, :, at] = (
             density[:, j * 128 : (j + 1) * 128].astype(F32) * jnp.where(low, a, b)
         ).astype(BF)
+    pl.semaphore_wait(barrier, peers + 1)
+
+    for n in needs[0] + needs[1]:
+        send_den(n)
     widen(0)
     load(1).start()
     for k in range(LEAD):
         arrange(k)
-
-    barrier = pltpu.get_barrier_semaphore()
-
-    @pl.loop(1, peers)
-    def _(p):
-        pr, pc = peer(p)
-        pl.semaphore_signal(barrier, inc=1, device_id=(pr, pc, dep), device_id_type=MESH)
-
-    pl.semaphore_signal(barrier, inc=1, device_id=(row, col, left), device_id_type=MESH)
-    pl.semaphore_signal(barrier, inc=1, device_id=(row, col, right), device_id_type=MESH)
-    pl.semaphore_wait(barrier, peers + 1)
-
-    for k in range(LEAD):
-        for n in needs[k]:
-            send_den(n)
         send(k)
     for n in needs[0]:
         share_den(n)
 
-    @pl.loop(0, chunks + hops)
+    @pl.loop(0, hops + 1)
     def _(i):
         for t in range(hops, -1, -1):
             if t == 0:
@@ -252,6 +250,18 @@
             def _(s=s):
                 for n in needs[s]:
                     share_den(n)
+
+    @pl.loop(hops + 1, chunks + hops)
+    def _(i):
+        for t in range(hops + 1):
+            if t == 0:
+                @pl.when(i + LEAD < chunks)
+                def _():
+                    prepare(i + LEAD)
+
+            @pl.when((i - t >= 0) & (i - t < chunks))
+            def _(t=t):
+                stage(i - t, t)
 
     sent(chunks - 1)
     rest = pl.ds(0, (n_col - 1) * nu)

time: 196 us -> 190 us (0.969)
  Pallas kernels: 194 us -> 189 us
    pallas_call x1, Pallas kernels: 194 us -> 189 us  [body(): pl.pallas_call(functools.partial(kernel, n_row, n_col, n_dep), out_shape=...]
where the time goes in v3:
time: 190 us
  Pallas kernels  189 us (99%)
    pallas_call x1, Pallas kernels, body(): pl.pallas_call(functools.partial(kernel, n_row, n_col, n_dep), out_shape=...  189 us

profile of v3, /device:TPU:1, one launch (start us, length us, event | category | flops | bytes accessed | tf_op | source)
XLA Modules:
  0.0 189.9 jit_solution(7118058334497143468)
XLA Ops:
  0.0 188.5 %shard_map.46 = bf16[128,64,128]{2,1,0:T(8,128)(2,1)S(1)} custom-call(bf16[16,2,64,2048]{3,2,1,0:T(8,128)(2,1)} %bitcast.3, bf16[16,1024]{1,0:T(8,128)(2,1)} %density.1, s32[2,32,64]{2,1,0:T(8,128)} %bitcast.4, s32[16,64]{1,0:T(8,128)} %bitcast.5), custom_call_target="tpu_custom_call" | custom-call | tf_op jit(solution)/shard_map/pallas_call | solution.py:282
  188.5 1.3 copy.6

commit v4 on v3

--- a/solution.py
+++ b/solution.py
@@ -58,7 +58,7 @@
                 b = tmask[h, 2 * c + 1, nu_block].astype(F32)
                 keep = jnp.where(low, a, b)[:1][None]
                 part = raw[:, h, :, lanes].astype(F32) * keep
-                wide[h, c] = part.reshape(nu * GROUP, q_dev)
+                wide[h, c, : nu * GROUP] = part.reshape(nu * GROUP, q_dev)
 
     def arrange(k):
         at = lax.rem(k, per_group) * MC
@@ -251,6 +251,11 @@
                 for n in needs[s]:
                     share_den(n)
 
+    rest = pl.ds(0, (n_col - 1) * nu)
+    for n in range(n_dep):
+        pltpu.make_async_copy(den.at[0, rest], den.at[0, rest], den_send.at[n]).wait()
+        sibling(n).wait_send()
+
     @pl.loop(hops + 1, chunks + hops)
     def _(i):
         for t in range(hops + 1):
@@ -264,10 +269,6 @@
                 stage(i - t, t)
 
     sent(chunks - 1)
-    rest = pl.ds(0, (n_col - 1) * nu)
-    for n in range(n_dep):
-        pltpu.make_async_copy(den.at[0, rest], den.at[0, rest], den_send.at[n]).wait()
-        sibling(n).wait_send()
 
 
 def solution(mesh):
@@ -286,7 +287,7 @@
             out_specs=vmem,
             scratch_shapes=[
                 pltpu.VMEM((nu, n_row, GROUP, aux), BF),
-                pltpu.VMEM((n_row, n_col, nu * GROUP, q_dev), F32),
+                pltpu.VMEM((n_row, n_col, (nu + 1) * GROUP, q_dev), F32),
                 pltpu.VMEM((chunks, n_row, n_col, nu, width), BF),
                 pltpu.VMEM((chunks, plane, width), BF),
                 pltpu.VMEM((chunks, hops, per_dev, width), BF),
@@ -295,7 +296,7 @@
                 pltpu.VMEM((n_dep, nu, per_dev), BF),
                 pltpu.VMEM((n_dep, plane, per_dev), BF),
                 pltpu.VMEM((n_dep, per_dev, plane), BF),
-                pltpu.VMEM((per_dev * GROUP, q_dev), F32),
+                pltpu.VMEM(((per_dev + 1) * GROUP, q_dev), F32),
                 pltpu.SemaphoreType.DMA,
                 pltpu.SemaphoreType.DMA((n_dep,)),
                 pltpu.SemaphoreType.DMA((n_dep,)),

time: 190 us -> 190 us (level)
  no operation moved by 1% of the time
where the time goes in v4:
time: 190 us
  Pallas kernels  189 us (99%)
    pallas_call x1, Pallas kernels, body(): pl.pallas_call(functools.partial(kernel, n_row, n_col, n_dep), out_shape=...  189 us

profile of v4, /device:TPU:1, one launch (start us, length us, event | category | flops | bytes accessed | tf_op | source)
XLA Modules:
  0.0 189.8 jit_solution(13023545183466809175)
XLA Ops:
  0.0 188.5 %shard_map.46 = bf16[128,64,128]{2,1,0:T(8,128)(2,1)S(1)} custom-call(bf16[16,2,64,2048]{3,2,1,0:T(8,128)(2,1)} %bitcast.3, bf16[16,1024]{1,0:T(8,128)(2,1)} %density.1, s32[2,32,64]{2,1,0:T(8,128)} %bitcast.4, s32[16,64]{1,0:T(8,128)} %bitcast.5), custom_call_target="tpu_custom_call" | custom-call | tf_op jit(solution)/shard_map/pallas_call | solution.py:283
  188.5 1.3 copy.6
